TPU v7x, 32 devices: a whole 2x2x4 slice. The times are simulated.
32 devices in a mesh: seq: 8 (over y, x, core), head: 4 (over z).
Axes of the slice: x: 2, y: 2, z: 4, core: 2. Of those that a mesh axis runs over, the one named last changes fastest.
Arguments:
- qkv: bfloat16 [4096, 4096], P(('seq', 'head')), may hold values from -24 to 24
- residual: bfloat16 [4096, 2048], P(('seq', 'head')), may hold values from -1.5 to 1.5
- dest_row: int32 [4096], P(('seq', 'head')), may hold values from 0 to 4095, as said below
- source_row: int32 [4096], P(('seq', 'head')), may hold values from 0 to 4095, as said below
- doc_start: int32 [4096], P('seq'), may hold values from 0 to 511, as said below
- out_weight: bfloat16 [3072, 2048], P('head'), may hold values from -0.109375 to 0.109375
- norm_gain: float32 [2048], replicated, may hold values from 0.5 to 1.5
Outputs:
- new_residual: bfloat16 [4096, 2048], P(('seq', 'head'))
- normed: bfloat16 [4096, 2048], P(('seq', 'head'))
Inputs may be any that keep to these rules, and one draw needn't show every extreme that they name: `dest_row`: A permutation of all rows. Row (s * 4 + h) * 128 + r goes to a place (g * 4 + h) * 128 + p with the same h. Of the 128 rows of one device, at most 24 go to one group g, every device sends exactly 24 rows to at least one group, and every device receives exactly 24 rows from at least one sender. `source_row`: the inverse permutation of dest_row. Documents are runs of consecutive rows inside one group: doc_start of a row is at most its own group-local index and equals that of the previous row unless the row begins a document; the first row of a group begins a document.
All inputs are finite; a program needn't handle non-finite values.
Results may differ from a plain program's by a relative error of at most 0.014.
Values may be sent and summed in bfloat16 or wider, within the bound.
A program may use at most 64 MiB of HBM per device.

v0:
```python
import jax
import jax.numpy as jnp
import numpy as np
from jax import lax
from jax.sharding import PartitionSpec as P

QH = 24
KVH = 4
HD = 128


def earlier_count(labels, order_keys):
    same = labels[:, None] == labels[None, :]
    before = order_keys[None, :] < order_keys[:, None]
    return jnp.sum((same & before).astype(jnp.int32), axis=1)


def local(qkv, residual, dest_row, source_row, doc_start, out_weight, norm_gain):
    n_seq = lax.axis_size("seq")
    n_head = lax.axis_size("head")
    tok_rows = qkv.shape[0]
    full_width = qkv.shape[1]
    capacity = max(2, 3 * tok_rows // (2 * n_seq))
    group_rows = tok_rows * n_head
    heads_here = out_weight.shape[0] // HD
    shared = QH // KVH
    qwidth = QH * HD
    kwidth = KVH * HD
    slots_all = jnp.arange(n_seq * capacity, dtype=jnp.int32)
    target = dest_row // group_rows
    local_order = jnp.arange(tok_rows, dtype=jnp.int32)
    send_slot = target * capacity + earlier_count(target, local_order)
    placing = (send_slot[None, :] == slots_all[:, None]).astype(jnp.bfloat16)
    outgoing = jnp.dot(placing, qkv, preferred_element_type=jnp.float32).astype(jnp.bfloat16)
    incoming = lax.all_to_all(
        outgoing.reshape(n_seq, capacity, full_width),
        "seq",
        split_axis=0,
        concat_axis=0,
        tiled=True,
    )
    sender = source_row // group_rows
    recv_slot = sender * capacity + earlier_count(sender, source_row)
    rows = jnp.take(incoming.reshape(n_seq * capacity, full_width), recv_slot, axis=0)
    query = rows[:, :qwidth].reshape(tok_rows, n_head, heads_here, HD)
    keys = rows[:, qwidth : qwidth + kwidth].reshape(tok_rows, KVH, HD)
    values = rows[:, qwidth + kwidth :].reshape(tok_rows, KVH, HD)
    kv_index = np.arange(n_head) * heads_here // shared
    kv_send = jnp.stack(
        [jnp.take(keys, kv_index, axis=1), jnp.take(values, kv_index, axis=1)], axis=2
    )
    q_group, kv_group = (
        lax.all_to_all(query, "head", split_axis=1, concat_axis=0, tiled=True),
        lax.all_to_all(kv_send, "head", split_axis=1, concat_axis=0, tiled=True),
    )
    queries = q_group.reshape(group_rows, heads_here, HD)
    group_keys = kv_group[:, 0, 0]
    group_values = kv_group[:, 0, 1]
    places = jnp.arange(group_rows, dtype=jnp.int32)
    block = min(group_rows, max(512, group_rows // 8))
    scale = HD ** (-0.5)
    pieces = []
    for index in range(group_rows // block):
        lower = index * block
        upper = lower + block
        scores = (
            jnp.einsum(
                "qhd,kd->hqk",
                queries[lower:upper],
                group_keys[:upper],
                preferred_element_type=jnp.float32,
            )
            * scale
        )
        qplace = places[lower:upper]
        kplace = places[:upper]
        visible = (kplace[None, :] <= qplace[:, None]) & (
            kplace[None, :] >= doc_start[lower:upper][:, None]
        )
        top = jnp.max(jnp.where(visible[None], scores, -1e30), axis=-1, keepdims=True)
        weights = jnp.where(visible[None], jnp.exp(scores - top), 0.0)
        total = jnp.sum(weights, axis=-1, keepdims=True)
        probs = weights.astype(jnp.bfloat16)
        numer = jnp.einsum(
            "hqk,kd->qhd", probs, group_values[:upper], preferred_element_type=jnp.float32
        )
        result = numer / jnp.transpose(total, (1, 0, 2))
        pieces.append(result.astype(jnp.bfloat16).reshape(block, heads_here * HD))
    attn = jnp.concatenate(pieces, axis=0)
    proj = lax.psum_scatter(
        jnp.dot(attn, out_weight, preferred_element_type=jnp.float32).astype(jnp.bfloat16),
        "head",
        scatter_dimension=0,
        tiled=True,
    )
    returning = (recv_slot[None, :] == slots_all[:, None]).astype(jnp.bfloat16)
    back_buffer = jnp.dot(returning, proj, preferred_element_type=jnp.float32).astype(jnp.bfloat16)
    arrived = lax.all_to_all(
        back_buffer.reshape(n_seq, capacity, proj.shape[1]),
        "seq",
        split_axis=0,
        concat_axis=0,
        tiled=True,
    )
    mine = jnp.take(arrived.reshape(n_seq * capacity, proj.shape[1]), send_slot, axis=0)
    new_residual = (residual.astype(jnp.float32) + mine.astype(jnp.float32)).astype(jnp.bfloat16)
    stream = lax.optimization_barrier(new_residual).astype(jnp.float32)
    factor = lax.rsqrt(jnp.mean(stream * stream, axis=-1, keepdims=True) + 1e-06)
    normed = (stream * factor * norm_gain).astype(jnp.bfloat16)
    return (new_residual, normed)


def solution(mesh):
    return jax.shard_map(
        local,
        mesh=mesh,
        in_specs=(
            P(("seq", "head"), None),
            P(("seq", "head"), None),
            P(("seq", "head")),
            P(("seq", "head")),
            P("seq"),
            P("head", None),
            P(),
        ),
        out_specs=(P(("seq", "head"), None), P(("seq", "head"), None)),
        check_vma=False,
    )
```

profile of v0, /device:TPU:0, one launch (start us, length us, event | category | flops | bytes accessed | tf_op | source)
XLA Modules:
  0.0 172.9 jit_solution(12865547734498911913)
XLA Ops:
  7.2 0.8 and_select_fusion.1
  8.2 0.7 compare_and_fusion.1
  8.9 2.9 %convolution_convert_fusion = bf16[192,4096]{1,0:T(8,128)(2,1)} fusion(bf16[128,4096]{1,0:T(8,128)(2,1)} %param.10, s32[128]{0:T(128)S(1)} %get-tuple-element.4), kind=kOutput, calls=%fused_computation.11 | convolution fusion | flops 202137600 | bytes 2621952 | tf_op jit(solution)/shard_map/dot_general | solution.py:34
  11.8 5.2 %all-to-all-start = ((bf16[8,24,4096]{2,1,0:T(8,128)(2,1)}), bf16[8,24,4096]{2,1,0:T(8,128)(2,1)}, u32[]{:S(2)}, u32[]{:S(2)}) async-start(bf16[8,24,4096]{2,1,0:T(8,128)(2,1)} %bitcast.79), calls=%async_computation | async-start | bytes 3145728 | tf_op jit(solution)/shard_map/all_to_all | solution.py:35
  17.0 0.5 broadcast_compare_fusion
  17.8 20.4 %all-to-all-done = bf16[8,24,4096]{2,1,0:T(8,128)(2,1)} async-done(((bf16[8,24,4096]{2,1,0:T(8,128)(2,1)}), bf16[8,24,4096]{2,1,0:T(8,128)(2,1)}, u32[]{:S(2)}, u32[]{:S(2)}) %all-to-all-start) | async-done | bytes 1572896 | tf_op jit(solution)/shard_map/all_to_all | solution.py:35
  38.1 4.8 %gather_fusion = bf16[128,4096]{1,0:T(8,128)(2,1)} fusion(bf16[192,4096]{1,0:T(8,128)(2,1)} %bitcast.1, s32[1024]{0:T(1024)S(1)} %pad_clamp_fusion.2), kind=kCustom, calls=%fused_computation.2 | custom fusion | bytes 2097664 | tf_op jit(solution)/shard_map/jit(_take)/gather | solution.py:44
  42.9 1.4 broadcast_select_fusion
  44.3 1.0 copy-done.2
  45.4 0.6 gather_fusion.2
  45.9 0.6 gather_fusion.3
  46.5 0.8 select_bitcast_fusion.1
  47.3 0.7 copy.29
  48.0 5.3 %all-to-all-start.1 = ((bf16[128,4,2,128]{3,0,2,1:T(8,128)(2,1)}), bf16[128,4,2,128]{3,0,2,1:T(8,128)(2,1)S(1)}, u32[]{:S(2)}, u32[]{:S(2)}) async-start(bf16[128,4,2,128]{3,0,2,1:T(8,128)(2,1)} %copy.29), calls=%async_computation.1 | async-start | bytes 524288 | tf_op jit(solution)/shard_map/all_to_all | solution.py:54
  53.4 2.1 %slice.32 = bf16[128,3072]{1,0:T(8,128)(2,1)} slice(bf16[128,4096]{1,0:T(8,128)(2,1)} %copy-done.2), slice={[0:128], [0:3072]} | slice | bytes 1572864 | tf_op jit(solution)/shard_map/slice | solution.py:45
  55.5 2.3 %copy.31 = bf16[128,3072]{0,1:T(8,128)(2,1)} copy(bf16[128,3072]{1,0:T(8,128)(2,1)} %slice.32) | data formatting | bytes 1572864 | tf_op jit(solution)/shard_map/slice | solution.py:45
  57.8 2.4 %all-to-all-done.1 = bf16[128,4,2,128]{3,0,2,1:T(8,128)(2,1)S(1)} async-done(((bf16[128,4,2,128]{3,0,2,1:T(8,128)(2,1)}), bf16[128,4,2,128]{3,0,2,1:T(8,128)(2,1)S(1)}, u32[]{:S(2)}, u32[]{:S(2)}) %all-to-all-start.1) | async-done | bytes 262176 | tf_op jit(solution)/shard_map/all_to_all | solution.py:54
  60.2 4.2 %all-to-all-start.2 = ((bf16[128,4,6,128]{0,3,2,1:T(8,128)(2,1)}), bf16[128,4,6,128]{0,3,2,1:T(8,128)(2,1)}, u32[]{:S(2)}, u32[]{:S(2)}) async-start(bf16[128,4,6,128]{0,3,2,1:T(8,128)(2,1)} %bitcast.80), calls=%async_computation.2 | async-start | bytes 1572864 | tf_op jit(solution)/shard_map/all_to_all | solution.py:53
  64.4 0.8 fusion.16
  65.2 0.7 copy.30
  66.0 14.4 %all-to-all-done.2 = bf16[128,4,6,128]{0,3,2,1:T(8,128)(2,1)} async-done(((bf16[128,4,6,128]{0,3,2,1:T(8,128)(2,1)}), bf16[128,4,6,128]{0,3,2,1:T(8,128)(2,1)}, u32[]{:S(2)}, u32[]{:S(2)}) %all-to-all-start.2) | async-done | bytes 786464 | tf_op jit(solution)/shard_map/all_to_all | solution.py:53
  80.4 2.3 %copy.32 = bf16[4,128,1,6,128]{4,1,0,3,2:T(8,128)(2,1)} copy(bf16[4,128,1,6,128]{1,4,3,0,2:T(8,128)(2,1)} %bitcast.15) | data formatting | bytes 1572864 | tf_op jit(solution)/shard_map/all_to_all | solution.py:53
  82.7 6.2 %fusion.25 = (f32[6,512]{1,0:T(8,128)S(1)}, bf16[6,512,512]{1,2,0:T(8,128)(2,1)}) fusion(pred[512,512]{0,1:T(8,128)(4,1)} %fusion.16, bf16[512,6,128]{2,0,1:T(8,128)(2,1)} %bitcast.83, bf16[512,1,2,128]{3,0,2,1:T(8,128)(2,1)} %bitcast.85), kind=kOutput, calls=%fused_computation.71 | convolution fusion | flops 816316928 | bytes 5517312 | tf_op jit(solution)/shard_map/sub | solution.py:81
  88.9 2.5 %fusion.10 = bf16[512,6,128]{0,2,1:T(8,128)(2,1)S(1)} fusion(bf16[6,512,512]{1,2,0:T(8,128)(2,1)} %get-tuple-element.12, f32[512,6]{0,1:T(8,128)S(1)} %bitcast.87, bf16[512,1,2,128]{3,0,2,1:T(8,128)(2,1)S(1)} %bitcast.86), kind=kOutput, calls=%fused_computation.20 | convolution fusion | flops 403439616 | bytes 4079616 | tf_op jit(solution)/shard_map/hqk,kd->qhd/dot_general | solution.py:84
  91.4 3.2 %convolution_convert_fusion.1 = bf16[512,2048]{1,0:T(8,128)(2,1)} fusion(bf16[512,768]{0,1:T(8,128)(2,1)S(1)} %bitcast.84, bf16[768,2048]{1,0:T(8,128)(2,1)S(1)} %copy-done), kind=kOutput, calls=%fused_computation.17 | convolution fusion | flops 1611661312 | bytes 6029312 | tf_op jit(solution)/shard_map/dot_general | solution.py:91
  94.6 46.2 %reduce-scatter.2.cloned.1.call-done = bf16[128,2048]{1,0:T(8,128)(2,1)} async-done(((bf16[512,2048]{1,0:T(8,128)(2,1)}), bf16[128,2048]{1,0:T(8,128)(2,1)}) %reduce-scatter.2.cloned.1.call-update) | async-done | bytes 524304 | tf_op jit(solution)/shard_map/reduce_scatter | solution.py:90
  140.8 2.3 %convolution_convert_fusion.2 = bf16[192,2048]{1,0:T(8,128)(2,1)} fusion(bf16[128,2048]{1,0:T(8,128)(2,1)} %reduce-scatter.2.cloned.1.call-done, s32[128]{0:T(128)S(1)} %get-tuple-element.6), kind=kOutput, calls=%fused_computation.18 | convolution fusion | flops 101081088 | bytes 1311232 | tf_op jit(solution)/shard_map/dot_general | solution.py:97
  143.1 4.2 %all-to-all-start.3 = ((bf16[8,24,2048]{2,1,0:T(8,128)(2,1)}), bf16[8,24,2048]{2,1,0:T(8,128)(2,1)}, u32[]{:S(2)}, u32[]{:S(2)}) async-start(bf16[8,24,2048]{2,1,0:T(8,128)(2,1)} %bitcast.81), calls=%async_computation.4 | async-start | bytes 1572864 | tf_op jit(solution)/shard_map/all_to_all | solution.py:98
  147.3 12.6 %all-to-all-done.3 = bf16[8,24,2048]{2,1,0:T(8,128)(2,1)} async-done(((bf16[8,24,2048]{2,1,0:T(8,128)(2,1)}), bf16[8,24,2048]{2,1,0:T(8,128)(2,1)}, u32[]{:S(2)}, u32[]{:S(2)}) %all-to-all-start.3) | async-done | bytes 786464 | tf_op jit(solution)/shard_map/all_to_all | solution.py:98
  159.9 3.5 %gather_fusion.1 = bf16[128,2048]{1,0:T(8,128)(2,1)} fusion(bf16[192,2048]{1,0:T(8,128)(2,1)} %bitcast.24, s32[1024]{0:T(1024)S(1)} %pad_clamp_fusion), kind=kCustom, calls=%fused_computation.3 | custom fusion | bytes 1049088 | tf_op jit(solution)/shard_map/jit(_take)/gather | solution.py:105
  163.4 1.4 add_convert_fusion
  165.1 1.0 fusion.15
  (30 shorter events, 0.8 us)
Async XLA Ops:
  7.2 84.2 %copy-start = (bf16[768,2048]{1,0:T(8,128)(2,1)S(1)}, bf16[768,2048]{1,0:T(8,128)(2,1)}, u32[]{:S(2)}) copy-start(bf16[768,2048]{1,0:T(8,128)(2,1)} %param.15) | copy-start | bytes 9437188
  7.2 10.3 %copy-start.5 = (s32[128]{0:T(128)S(1)}, s32[128]{0:T(128)}, u32[]{:S(2)}) copy-start(s32[128]{0:T(128)} %param.13) | copy-start | bytes 1540
  11.8 26.3 %all-to-all-start = ((bf16[8,24,4096]{2,1,0:T(8,128)(2,1)}), bf16[8,24,4096]{2,1,0:T(8,128)(2,1)}, u32[]{:S(2)}, u32[]{:S(2)}) async-start(bf16[8,24,4096]{2,1,0:T(8,128)(2,1)} %bitcast.79), calls=%async_computation | async-start | bytes 3145728 | tf_op jit(solution)/shard_map/all_to_all | solution.py:35
  44.3 1.0 copy-start.2
  47.3 17.1 %copy-start.6 = (s32[512]{0:T(512)S(1)}, s32[512]{0:T(512)}, u32[]{:S(2)}) copy-start(s32[512]{0:T(512)} %param.14) | copy-start | bytes 6148
  48.0 12.1 %all-to-all-start.1 = ((bf16[128,4,2,128]{3,0,2,1:T(8,128)(2,1)}), bf16[128,4,2,128]{3,0,2,1:T(8,128)(2,1)S(1)}, u32[]{:S(2)}, u32[]{:S(2)}) async-start(bf16[128,4,2,128]{3,0,2,1:T(8,128)(2,1)} %copy.29), calls=%async_computation.1 | async-start | bytes 524288 | tf_op jit(solution)/shard_map/all_to_all | solution.py:54
  60.2 20.2 %all-to-all-start.2 = ((bf16[128,4,6,128]{0,3,2,1:T(8,128)(2,1)}), bf16[128,4,6,128]{0,3,2,1:T(8,128)(2,1)}, u32[]{:S(2)}, u32[]{:S(2)}) async-start(bf16[128,4,6,128]{0,3,2,1:T(8,128)(2,1)} %bitcast.80), calls=%async_computation.2 | async-start | bytes 1572864 | tf_op jit(solution)/shard_map/all_to_all | solution.py:53
  64.3 76.5 %reduce-scatter.2.cloned.1.call-start = ((), (), s32[]{:S(2)}) async-start(), calls=%async_computation.5 | async-start | bytes 2621440 | tf_op jit(solution)/shard_map/reduce_scatter | solution.py:90
  82.7 6.2 %copy-start.3 = (bf16[4,128,1,2,128]{4,1,0,3,2:T(8,128)(2,1)S(1)}, bf16[4,128,1,2,128]{4,1,0,3,2:T(8,128)(2,1)}, u32[]{:S(2)}) copy-start(bf16[4,128,1,2,128]{4,1,0,3,2:T(8,128)(2,1)} %copy.30) | copy-start | bytes 786436
  143.1 16.8 %all-to-all-start.3 = ((bf16[8,24,2048]{2,1,0:T(8,128)(2,1)}), bf16[8,24,2048]{2,1,0:T(8,128)(2,1)}, u32[]{:S(2)}, u32[]{:S(2)}) async-start(bf16[8,24,2048]{2,1,0:T(8,128)(2,1)} %bitcast.81), calls=%async_computation.4 | async-start | bytes 1572864 | tf_op jit(solution)/shard_map/all_to_all | solution.py:98
  159.9 5.1 %copy-start.4 = (f32[2048]{0:T(1024)S(1)}, f32[2048]{0:T(1024)}, u32[]{:S(2)}) copy-start(f32[2048]{0:T(1024)} %param.16) | copy-start | bytes 24580
  164.8 1.2 copy-start.1
Sparse Core Ops, SparseCore 0:
  94.7 46.0 reduce-scatter.1
where the time goes:
time: 174 us; the launch traced here: 173 us
  waiting for transfers between devices  96 us (55%)
  starting transfers between devices  19 us (11%)
  local copies, waits for them, and re-layouts  18.6 us (11%)
  matrix products  17.1 us (10%)
  between operations  14.2 us (8%)
  other arithmetic  8.02 us (5%)
    reduce_scatter x1, waiting for transfers between devices, local(): lax.psum_scatter(jnp.dot(attn, out_weight, preferred_element_type=jnp.flo...  46.2 us
    all_to_all x1, waiting for transfers between devices, local(): lax.all_to_all(outgoing.reshape(n_seq, capacity, full_width), 'seq', spli...  20.4 us
    all_to_all x1, waiting for transfers between devices, local(): lax.all_to_all(query, 'head', split_axis=1, concat_axis=0, tiled=True)  14.4 us
    all_to_all x1, waiting for transfers between devices, local(): lax.all_to_all(back_buffer.reshape(n_seq, capacity, proj.shape[1]), 'seq'...  12.6 us
    sub x1, matrix products, local(): weights = jnp.where(visible[None], jnp.exp(scores - top), 0.0)  6.17 us
    all_to_all x1, starting transfers between devices, local(): lax.all_to_all(kv_send, 'head', split_axis=1, concat_axis=0, tiled=True)  5.34 us
    all_to_all x1, starting transfers between devices, local(): lax.all_to_all(outgoing.reshape(n_seq, capacity, full_width), 'seq', spli...  5.17 us
    gather x1, local copies, waits for them, and re-layouts, local(): jnp.take(incoming.reshape(n_seq * capacity, full_width), recv_slot, axis=0)  4.8 us
  transfers between devices with their start and end apart: 5, of which 5 were waited for; matrix products, arithmetic and copies ran while one was open for 4% of the time, Pallas kernels for 0%

commit v1 on v0

v1 whole, which is shorter than its diff:
```python
import functools

import jax
import jax.numpy as jnp
import numpy as np
from jax import lax
from jax.experimental import pallas as pl
from jax.experimental.pallas import tpu as pltpu
from jax.sharding import PartitionSpec as P

QH = 24
KVH = 4
HD = 128
MESH = pl.DeviceIdType.MESH


def one_hot_slots(member, ranks, n_seq, cap):
    rows = member.shape[1]
    rank = jnp.where(member, ranks.astype(jnp.int32), -4 * cap)
    place = lax.broadcasted_iota(jnp.int32, (n_seq, 2 * cap, rows), 1)
    low = (rank[:, None, :] == place).astype(jnp.float32).reshape(n_seq * 2 * cap, rows)
    high = (rank[:, None, :] + cap == place).astype(jnp.float32).reshape(n_seq * 2 * cap, rows)
    return low, high


def kernel(
    n_seq, n_head, cap, jobs,
    qkv, residual, dest, source, starts, weight, gain,
    out_res, out_norm,
    w_vmem, p_one, pt_one, r_one, rt_one, x_send, x_recv, z_send, z_recv, attn,
    s_send, s_recv, acc, b_send, b_recv,
    w_sem, xs_sem, xr_sem, zs_sem, zr_sem, ss_sem, sr_sem, bs_sem, br_sem,
):
    f32, bf16 = jnp.float32, jnp.bfloat16
    seq, head = lax.axis_index("seq"), lax.axis_index("head")
    tok = qkv.shape[0]
    group = tok * n_head
    heads_here = weight.shape[0] // HD
    shared = QH // KVH
    width = x_send.shape[3] * 2
    half = width // 2
    cols = weight.shape[1] // jobs
    slots = n_seq * 2 * cap

    def dot(a, b):
        return jnp.dot(a, b, preferred_element_type=f32)

    def wait_bytes(ref, sem):
        pltpu.make_async_copy(ref, ref, sem).wait()

    load_w = pltpu.make_async_copy(weight, w_vmem, w_sem)
    load_w.start()

    barrier = pltpu.get_barrier_semaphore()

    @pl.loop(1, n_seq)
    def _(i):
        pl.semaphore_signal(barrier, inc=1, device_id=((seq + i) % n_seq, head), device_id_type=MESH)

    @pl.loop(1, n_head)
    def _(i):
        pl.semaphore_signal(barrier, inc=1, device_id=(seq, (head + i) % n_head), device_id_type=MESH)

    bounds = lax.broadcasted_iota(jnp.int32, (n_seq, tok), 0) * group
    goes = (dest[...] >= bounds) & (dest[...] < bounds + group)
    comes = (source[...] >= bounds) & (source[...] < bounds + group)
    earlier = lax.broadcasted_iota(jnp.int32, (tok, tok), 0) < lax.broadcasted_iota(jnp.int32, (tok, tok), 1)
    low, high = one_hot_slots(goes, dot(goes.astype(f32).astype(bf16), earlier.astype(f32).astype(bf16)), n_seq, cap)
    p_one[0], p_one[1] = low.astype(bf16), high.astype(bf16)

    pl.semaphore_wait(barrier, n_seq + n_head - 2)

    shifts = sorted(range(n_head), key=lambda s: (s == 0, abs(s - n_head / 2), -s))
    for c, shift in enumerate(shifts):
        to = (head + shift) % n_head
        kv = (to * heads_here) // shared
        query = qkv[:, pl.ds(pl.multiple_of(to * heads_here * HD, HD), heads_here * HD)]
        key = qkv[:, pl.ds(pl.multiple_of(QH * HD + kv * HD, HD), HD)]
        value = qkv[:, pl.ds(pl.multiple_of((QH + KVH) * HD + kv * HD, HD), HD)]
        x = jnp.concatenate([query, key, value], axis=1)
        placed = (dot(p_one[0], x[:, :half]) + dot(p_one[1], x[:, half:])).astype(bf16)
        x_send[c] = placed.reshape(n_seq, 2 * cap, half)
        x_recv[c, pl.ds(seq, 1)] = x_send[c, pl.ds(seq, 1)]

        @pl.loop(1, n_seq)
        def _(i):
            peer = (seq + i) % n_seq
            pltpu.make_async_remote_copy(
                src_ref=x_send.at[c, peer], dst_ref=x_recv.at[c, seq],
                send_sem=xs_sem.at[c], recv_sem=xr_sem.at[c],
                device_id=(peer, head), device_id_type=MESH,
            ).start()

        if c == 0:
            pt_one[0], pt_one[1] = low.T.astype(bf16), high.T.astype(bf16)
            across = jnp.broadcast_to(source[...].astype(f32), (tok, tok))
            before = (across.T < across).astype(f32).astype(bf16)
            rlow, rhigh = one_hot_slots(comes, dot(comes.astype(f32).astype(bf16), before), n_seq, cap)
            r_one[0], r_one[1] = rlow.astype(bf16), rhigh.astype(bf16)
            rt_one[0], rt_one[1] = rlow.T.astype(bf16), rhigh.T.astype(bf16)

    for c, shift in enumerate(shifts):
        to = (head + shift) % n_head
        wait_bytes(x_recv.at[c, pl.ds(0, n_seq - 1)], xr_sem.at[c])
        arrived = x_recv[c].reshape(slots, half)
        rows = jnp.concatenate([dot(rt_one[0], arrived), dot(rt_one[1], arrived)], axis=1).astype(bf16)
        if shift == 0:
            z_recv[pl.ds(head, 1)] = rows[None]
        else:
            z_send[c] = rows
            pltpu.make_async_remote_copy(
                src_ref=z_send.at[c], dst_ref=z_recv.at[head],
                send_sem=zs_sem.at[c], recv_sem=zr_sem.at[head],
                device_id=(seq, to), device_id_type=MESH,
            ).start()

    @pl.loop(1, n_head)
    def _(i):
        other = (head + i) % n_head
        wait_bytes(z_recv.at[other], zr_sem.at[other])

    factor = HD ** (-0.5) * float(np.log2(np.e))
    kcol = heads_here * HD
    for i in range(n_head):
        span = (i + 1) * tok
        keys = z_recv[: i + 1, :, kcol : kcol + HD].reshape(span, HD)
        values = z_recv[: i + 1, :, kcol + HD : kcol + 2 * HD].reshape(span, HD)
        first = jnp.broadcast_to(starts[:, i * tok : (i + 1) * tok].astype(f32), (tok, tok)).T[:, :1]
        kplace = lax.broadcasted_iota(jnp.int32, (tok, span), 1)
        qplace = lax.broadcasted_iota(jnp.int32, (tok, span), 0) + i * tok
        visible = (kplace <= qplace) & (kplace >= first.astype(jnp.int32))
        for a in range(heads_here):
            scores = lax.dot_general(
                z_recv[i, :, a * HD : (a + 1) * HD], keys, (((1,), (1,)), ((), ())), preferred_element_type=f32
            )
            scores = jnp.where(visible, scores, -1e30)
            top = jnp.max(scores, axis=-1, keepdims=True)
            weights = jnp.exp2((scores - top) * factor)
            total = jnp.sum(weights, axis=-1, keepdims=True)
            attn[i, :, a * HD : (a + 1) * HD] = (dot(weights.astype(bf16), values) / total).astype(bf16)

    load_w.wait()

    def partial(block, j):
        return dot(attn[block], w_vmem[:, pl.ds(pl.multiple_of(j * cols, cols), cols)])

    @pl.loop(0, n_head - 1)
    def _(t):
        above, below = n_head - 1 - t, t

        @pl.loop(0, jobs)
        def _(j):
            @pl.when(above > head)
            def _():
                acc[...] = partial(above, j)

                @pl.when(head > 0)
                def _():
                    wait_bytes(s_recv.at[above + 1, j], sr_sem.at[above + 1, j])
                    acc[...] += s_recv[above + 1, j].astype(f32)

                s_send[above, j] = acc[...].astype(bf16)
                pltpu.make_async_remote_copy(
                    src_ref=s_send.at[above, j], dst_ref=s_recv.at[above + 1, j],
                    send_sem=ss_sem.at[above, j], recv_sem=sr_sem.at[above + 1, j],
                    device_id=(seq, head + 1), device_id_type=MESH,
                ).start()

            @pl.when(below < head)
            def _():
                acc[...] = partial(below, j)

                @pl.when(head < n_head - 1)
                def _():
                    wait_bytes(s_recv.at[below, j], sr_sem.at[below, j])
                    acc[...] += s_recv[below, j].astype(f32)

                s_send[below, j] = acc[...].astype(bf16)
                pltpu.make_async_remote_copy(
                    src_ref=s_send.at[below, j], dst_ref=s_recv.at[below, j],
                    send_sem=ss_sem.at[below, j], recv_sem=sr_sem.at[below, j],
                    device_id=(seq, head - 1), device_id_type=MESH,
                ).start()

    quarter = cols // 2

    @pl.loop(0, jobs)
    def _(j):
        acc[...] = partial(head, j)

        @pl.when(head > 0)
        def _():
            wait_bytes(s_recv.at[head + 1, j], sr_sem.at[head + 1, j])
            acc[...] += s_recv[head + 1, j].astype(f32)

        @pl.when(head < n_head - 1)
        def _():
            wait_bytes(s_recv.at[head, j], sr_sem.at[head, j])
            acc[...] += s_recv[head, j].astype(f32)

        proj = acc[...].astype(bf16)
        back = (dot(r_one[0], proj[:, :quarter]) + dot(r_one[1], proj[:, quarter:])).astype(bf16)
        b_send[j] = back.reshape(n_seq, 2 * cap, quarter)
        b_recv[j, pl.ds(seq, 1)] = b_send[j, pl.ds(seq, 1)]

        @pl.loop(1, n_seq)
        def _(i):
            peer = (seq + i) % n_seq
            pltpu.make_async_remote_copy(
                src_ref=b_send.at[j, peer], dst_ref=b_recv.at[j, seq],
                send_sem=bs_sem.at[j], recv_sem=br_sem.at[j],
                device_id=(peer, head), device_id_type=MESH,
            ).start()

    square = jnp.zeros((tok, 1), f32)
    for j in range(jobs):
        wait_bytes(b_recv.at[j, pl.ds(0, n_seq - 1)], br_sem.at[j])
        arrived = b_recv[j].reshape(slots, quarter)
        mine = jnp.concatenate([dot(pt_one[0], arrived), dot(pt_one[1], arrived)], axis=1)
        here = slice(j * cols, (j + 1) * cols)
        stream = (residual[:, here].astype(f32) + mine).astype(bf16)
        out_res[:, here] = stream
        wide = stream.astype(f32)
        square += jnp.sum(wide * wide, axis=-1, keepdims=True)
    scale = lax.rsqrt(square / (jobs * cols) + 1e-06)
    for j in range(jobs):
        here = slice(j * cols, (j + 1) * cols)
        out_norm[:, here] = (out_res[:, here].astype(f32) * scale * gain[:, here]).astype(bf16)

    for c, shift in enumerate(shifts):
        wait_bytes(x_send.at[c, pl.ds(0, n_seq - 1)], xs_sem.at[c])
        if shift != 0:
            wait_bytes(z_send.at[c], zs_sem.at[c])

    @pl.loop(0, jobs)
    def _(j):
        wait_bytes(b_send.at[j, pl.ds(0, n_seq - 1)], bs_sem.at[j])

        @pl.loop(1, n_head)
        def _(i):
            block = (head + i) % n_head
            wait_bytes(s_send.at[block, j], ss_sem.at[block, j])


def local(qkv, residual, dest_row, source_row, doc_start, out_weight, norm_gain):
    n_seq = lax.axis_size("seq")
    n_head = lax.axis_size("head")
    tok, _ = qkv.shape
    depth, model = out_weight.shape
    cap = -(-max(2, 3 * tok // (2 * n_seq)) // 8) * 8
    jobs = 4
    width = depth + 2 * HD
    cols = model // jobs
    bf16 = jnp.bfloat16
    dma = pltpu.SemaphoreType.DMA
    vmem = pl.BlockSpec(memory_space=pltpu.VMEM)
    return pl.pallas_call(
        functools.partial(kernel, n_seq, n_head, cap, jobs),
        out_shape=(jax.ShapeDtypeStruct(residual.shape, bf16), jax.ShapeDtypeStruct(residual.shape, bf16)),
        in_specs=[vmem, vmem, vmem, vmem, vmem, pl.BlockSpec(memory_space=pl.ANY), vmem],
        out_specs=(vmem, vmem),
        scratch_shapes=[
            pltpu.VMEM((depth, model), bf16),
            pltpu.VMEM((2, n_seq * 2 * cap, tok), bf16),
            pltpu.VMEM((2, tok, n_seq * 2 * cap), bf16),
            pltpu.VMEM((2, n_seq * 2 * cap, tok), bf16),
            pltpu.VMEM((2, tok, n_seq * 2 * cap), bf16),
            pltpu.VMEM((n_head, n_seq, 2 * cap, width // 2), bf16),
            pltpu.VMEM((n_head, n_seq, 2 * cap, width // 2), bf16),
            pltpu.VMEM((n_head, tok, width), bf16),
            pltpu.VMEM((n_head, tok, width), bf16),
            pltpu.VMEM((n_head, tok, depth), bf16),
            pltpu.VMEM((n_head, jobs, tok, cols), bf16),
            pltpu.VMEM((n_head + 1, jobs, tok, cols), bf16),
            pltpu.VMEM((tok, cols), jnp.float32),
            pltpu.VMEM((jobs, n_seq, 2 * cap, cols // 2), bf16),
            pltpu.VMEM((jobs, n_seq, 2 * cap, cols // 2), bf16),
            dma,
            dma((n_head,)),
            dma((n_head,)),
            dma((n_head,)),
            dma((n_head,)),
            dma((n_head, jobs)),
            dma((n_head + 1, jobs)),
            dma((jobs,)),
            dma((jobs,)),
        ],
        compiler_params=pltpu.CompilerParams(
            collective_id=0, has_side_effects=True, vmem_limit_bytes=56 * 1024 * 1024
        ),
        name="layer",
    )(
        qkv,
        residual,
        dest_row.reshape(1, tok),
        source_row.reshape(1, tok),
        doc_start.reshape(1, tok * n_head),
        out_weight,
        norm_gain.reshape(1, model),
    )


def solution(mesh):
    return jax.shard_map(
        local,
        mesh=mesh,
        in_specs=(
            P(("seq", "head"), None),
            P(("seq", "head"), None),
            P(("seq", "head")),
            P(("seq", "head")),
            P("seq"),
            P("head", None),
            P(),
        ),
        out_specs=(P(("seq", "head"), None), P(("seq", "head"), None)),
        check_vma=False,
    )
```

time: 174 us -> 99.2 us (0.57)
  the two profiles are of different devices: /device:TPU:0 before, /device:TPU:11 now
where the time goes in v1:
time: 99.2 us; the launch traced here: 98 us
  Pallas kernels  93.6 us (94%)
  local copies, waits for them, and re-layouts  3.76 us (4%)
    pallas_call x1, Pallas kernels, local(): pl.pallas_call(functools.partial(kernel, n_seq, n_head, cap, jobs), out_s...  93.6 us
    unnamed x2, local copies, waits for them, and re-layouts  3.76 us

profile of v1, /device:TPU:11, one launch (start us, length us, event | category | flops | bytes accessed | tf_op | source)
XLA Modules:
  0.0 98.0 jit_solution(6492843490227844617)
XLA Ops:
  0.6 93.6 %layer.1 = (bf16[128,2048]{1,0:T(8,128)(2,1)}, bf16[128,2048]{1,0:T(8,128)(2,1)}) custom-call(bf16[128,4096]{1,0:T(8,128)(2,1)} %qkv.1, bf16[128,2048]{1,0:T(8,128)(2,1)} %residual.1, s32[1,128]{1,0:T(1,128)} %bitcast.6, s32[1,128]{1,0:T(1,128)} %bitcast.7, s32[1,512]{1,0:T(1,128)} %bitcast.5, bf16[768,2048]{1,0:T(8,128)(2,1)} %weight.1, f32[1,2048]{1,0:T(1,128)} %bitcast.4), custom_call_target="tpu_custom_call" | custom-call | tf_op jit(solution)/shard_map/layer/pallas_call | solution.py:257
  94.2 1.9 %copy.11 = bf16[128,2048]{1,0:T(8,128)(2,1)} copy(bf16[128,2048]{1,0:T(8,128)(2,1)} %get-tuple-element.4) | data formatting | bytes 1048576
  96.1 1.9 %copy.12 = bf16[128,2048]{1,0:T(8,128)(2,1)} copy(bf16[128,2048]{1,0:T(8,128)(2,1)} %get-tuple-element.5) | data formatting | bytes 1048576

commit v2 on v1

v2 whole, which is shorter than its diff:
```python
import functools

import jax
import jax.numpy as jnp
import numpy as np
from jax import lax
from jax.experimental import pallas as pl
from jax.experimental.pallas import tpu as pltpu
from jax.sharding import PartitionSpec as P

QH = 24
KVH = 4
HD = 128
MESH = pl.DeviceIdType.MESH


def one_hot_slots(member, ranks, n_seq, cap):
    rows = member.shape[1]
    rank = jnp.where(member, ranks.astype(jnp.int32), -4 * cap)
    place = lax.broadcasted_iota(jnp.int32, (n_seq, 2 * cap, rows), 1)
    low = (rank[:, None, :] == place).astype(jnp.float32).reshape(n_seq * 2 * cap, rows)
    high = (rank[:, None, :] + cap == place).astype(jnp.float32).reshape(n_seq * 2 * cap, rows)
    return low, high


def kernel(
    n_seq, n_head, cap, jobs,
    qkv, dest, source, starts, weight,
    out,
    w_vmem, p_one, pt_one, r_one, rt_one, kx_send, kx_recv, x_send, x_recv, kv_rows, k_send, kv_recv,
    z_send, q_recv, attn, s_send, s_recv, acc, b_send, b_recv,
    w_sem, kxs_sem, kxr_sem, xs_sem, xr_sem, ks_sem, kr_sem, zs_sem, zr_sem, ss_sem, sr_sem, bs_sem, br_sem,
):
    f32, bf16 = jnp.float32, jnp.bfloat16
    seq, head = lax.axis_index("seq"), lax.axis_index("head")
    tok = qkv.shape[0]
    group = tok * n_head
    heads_here = weight.shape[0] // HD
    shared = QH // KVH
    cols = weight.shape[1] // jobs
    slots = n_seq * 2 * cap

    def dot(a, b):
        return jnp.dot(a, b, preferred_element_type=f32)

    def wait_bytes(ref, sem):
        pltpu.make_async_copy(ref, ref, sem).wait()

    load_w = pltpu.make_async_copy(weight, w_vmem, w_sem)
    load_w.start()

    barrier = pltpu.get_barrier_semaphore()

    @pl.loop(1, n_seq)
    def _(i):
        pl.semaphore_signal(barrier, inc=1, device_id=((seq + i) % n_seq, head), device_id_type=MESH)

    @pl.loop(1, n_head)
    def _(i):
        pl.semaphore_signal(barrier, inc=1, device_id=(seq, (head + i) % n_head), device_id_type=MESH)

    bounds = lax.broadcasted_iota(jnp.int32, (n_seq, tok), 0) * group
    goes = (dest[...] >= bounds) & (dest[...] < bounds + group)
    comes = (source[...] >= bounds) & (source[...] < bounds + group)
    earlier = lax.broadcasted_iota(jnp.int32, (tok, tok), 0) < lax.broadcasted_iota(jnp.int32, (tok, tok), 1)
    low, high = one_hot_slots(goes, dot(goes.astype(f32).astype(bf16), earlier.astype(f32).astype(bf16)), n_seq, cap)
    p_one[0], p_one[1] = low.astype(bf16), high.astype(bf16)

    pl.semaphore_wait(barrier, n_seq + n_head - 2)

    def partner(c):
        if n_head == 4:
            mirror = n_head - 1 - head
            return [mirror, (head + 2) % n_head, (mirror + 2) % n_head, head][c]
        return (shifts[c] - head + n_head) % n_head

    def place(x, send, recv, s_sem, r_sem):
        side = x.shape[1] // 2
        placed = (dot(p_one[0], x[:, :side]) + dot(p_one[1], x[:, side:])).astype(bf16)
        send[...] = placed.reshape(n_seq, 2 * cap, side)
        recv[pl.ds(seq, 1)] = send[pl.ds(seq, 1)]

        @pl.loop(1, n_seq)
        def _(i):
            peer = (seq + i) % n_seq
            pltpu.make_async_remote_copy(
                src_ref=send.at[peer], dst_ref=recv.at[seq],
                send_sem=s_sem, recv_sem=r_sem,
                device_id=(peer, head), device_id_type=MESH,
            ).start()

    def gather(recv, r_sem):
        wait_bytes(recv.at[pl.ds(0, n_seq - 1)], r_sem)
        arrived = recv[...].reshape(slots, recv.shape[2])
        return jnp.concatenate([dot(rt_one[0], arrived), dot(rt_one[1], arrived)], axis=1).astype(bf16)

    shifts = [(n_head - 1 + c) % n_head for c in range(n_head)]
    depth = heads_here * HD
    place(qkv[:, QH * HD :], kx_send, kx_recv, kxs_sem, kxr_sem)

    low_t, high_t = low.T, high.T
    pt_one[0], pt_one[1] = low_t.astype(bf16), high_t.astype(bf16)
    across = jnp.broadcast_to(source[...].astype(f32), (tok, tok))
    before = (across.T < across).astype(f32).astype(bf16)
    rlow, rhigh = one_hot_slots(comes, dot(comes.astype(f32).astype(bf16), before), n_seq, cap)
    r_one[0], r_one[1] = rlow.astype(bf16), rhigh.astype(bf16)
    rt_one[0], rt_one[1] = rlow.T.astype(bf16), rhigh.T.astype(bf16)

    for c in range(n_head):
        query = qkv[:, pl.ds(pl.multiple_of(partner(c) * depth, HD), depth)]
        place(query, x_send.at[c], x_recv.at[c], xs_sem.at[c], xr_sem.at[c])

    kv_rows[...] = gather(kx_recv, kxr_sem)

    def kv_of(block):
        kv = (block * heads_here) // shared
        key = kv_rows[:, pl.ds(pl.multiple_of(kv * HD, HD), HD)]
        value = kv_rows[:, pl.ds(pl.multiple_of((KVH + kv) * HD, HD), HD)]
        return jnp.concatenate([key, value], axis=1)

    kv_recv[pl.ds(head, 1)] = kv_of(head)[None]
    for c in range(1, n_head):
        to = (head + c) % n_head
        k_send[c] = kv_of(to)
        pltpu.make_async_remote_copy(
            src_ref=k_send.at[c], dst_ref=kv_recv.at[head],
            send_sem=ks_sem.at[c], recv_sem=kr_sem.at[head],
            device_id=(seq, to), device_id_type=MESH,
        ).start()

    for c in range(n_head):
        rows = gather(x_recv.at[c], xr_sem.at[c])
        to = partner(c)
        z_send[c] = rows

        @pl.when(to == head)
        def _():
            q_recv[pl.ds(head, 1)] = z_send[pl.ds(c, 1)]

        @pl.when(to != head)
        def _():
            pltpu.make_async_remote_copy(
                src_ref=z_send.at[c], dst_ref=q_recv.at[head],
                send_sem=zs_sem.at[c], recv_sem=zr_sem.at[head],
                device_id=(seq, to), device_id_type=MESH,
            ).start()

    @pl.loop(1, n_head)
    def _(i):
        other = (head + i) % n_head
        wait_bytes(kv_recv.at[other], kr_sem.at[other])

    load_w.wait()
    factor = HD ** (-0.5) * float(np.log2(np.e))

    def attend(i):
        span = (i + 1) * tok
        keys = kv_recv[: i + 1, :, :HD].reshape(span, HD)
        values = kv_recv[: i + 1, :, HD:].reshape(span, HD)
        first = jnp.broadcast_to(starts[:, i * tok : (i + 1) * tok].astype(f32), (tok, tok)).T[:, :1]
        kplace = lax.broadcasted_iota(jnp.int32, (tok, span), 1)
        qplace = lax.broadcasted_iota(jnp.int32, (tok, span), 0) + i * tok
        visible = (kplace <= qplace) & (kplace >= first.astype(jnp.int32))
        for a in range(heads_here):
            scores = lax.dot_general(
                q_recv[i, :, a * HD : (a + 1) * HD], keys, (((1,), (1,)), ((), ())), preferred_element_type=f32
            )
            scores = jnp.where(visible, scores, -1e30)
            top = jnp.max(scores, axis=-1, keepdims=True)
            weights = jnp.exp2((scores - top) * factor)
            total = jnp.sum(weights, axis=-1, keepdims=True)
            attn[i, :, a * HD : (a + 1) * HD] = (dot(weights.astype(bf16), values) / total).astype(bf16)

    def partial(block, j):
        return dot(attn[block], w_vmem[:, pl.ds(pl.multiple_of(j * cols, cols), cols)])

    def step(block, j):
        up = block > head
        slot = jnp.where(up, block + 1, block)
        acc[...] = partial(block, j)

        @pl.when((head > 0) & (head < n_head - 1))
        def _():
            wait_bytes(s_recv.at[slot, j], sr_sem.at[slot, j])
            acc[...] += s_recv[slot, j].astype(f32)

        s_send[block, j] = acc[...].astype(bf16)
        pltpu.make_async_remote_copy(
            src_ref=s_send.at[block, j], dst_ref=s_recv.at[slot, j],
            send_sem=ss_sem.at[block, j], recv_sem=sr_sem.at[slot, j],
            device_id=(seq, jnp.where(up, head + 1, head - 1)), device_id_type=MESH,
        ).start()

    end = (head == 0) | (head == n_head - 1)

    @pl.loop(0, n_head)
    def _(t):
        block = partner(n_head - 1)
        for c in range(n_head - 1):
            block = jnp.where(t == c, partner(c), block)

        @pl.when(block != head)
        def _():
            wait_bytes(q_recv.at[block], zr_sem.at[block])

        for i in range(n_head):
            pl.when(block == i)(functools.partial(attend, i))

        @pl.when((block != head) & end)
        def _():
            @pl.loop(0, jobs)
            def _(j):
                step(block, j)

    @pl.when(jnp.logical_not(end))
    def _():
        @pl.loop(0, n_head - 1)
        def _(t):
            above, below = n_head - 1 - t, t

            @pl.loop(0, jobs)
            def _(j):
                @pl.when(above > head)
                def _():
                    step(above, j)

                @pl.when(below < head)
                def _():
                    step(below, j)

    quarter = cols // 2

    @pl.loop(0, jobs)
    def _(j):
        acc[...] = partial(head, j)

        @pl.when(head > 0)
        def _():
            wait_bytes(s_recv.at[head + 1, j], sr_sem.at[head + 1, j])
            acc[...] += s_recv[head + 1, j].astype(f32)

        @pl.when(head < n_head - 1)
        def _():
            wait_bytes(s_recv.at[head, j], sr_sem.at[head, j])
            acc[...] += s_recv[head, j].astype(f32)

        proj = acc[...].astype(bf16)
        back = (dot(r_one[0], proj[:, :quarter]) + dot(r_one[1], proj[:, quarter:])).astype(bf16)
        b_send[j] = back.reshape(n_seq, 2 * cap, quarter)
        b_recv[j, pl.ds(seq, 1)] = b_send[j, pl.ds(seq, 1)]

        @pl.loop(1, n_seq)
        def _(i):
            peer = (seq + i) % n_seq
            pltpu.make_async_remote_copy(
                src_ref=b_send.at[j, peer], dst_ref=b_recv.at[j, seq],
                send_sem=bs_sem.at[j], recv_sem=br_sem.at[j],
                device_id=(peer, head), device_id_type=MESH,
            ).start()

    for j in range(jobs):
        wait_bytes(b_recv.at[j, pl.ds(0, n_seq - 1)], br_sem.at[j])
        arrived = b_recv[j].reshape(slots, quarter)
        mine = jnp.concatenate([dot(pt_one[0], arrived), dot(pt_one[1], arrived)], axis=1)
        out[:, j * cols : (j + 1) * cols] = mine.astype(bf16)

    wait_bytes(kx_send.at[pl.ds(0, n_seq - 1)], kxs_sem)
    for c in range(n_head):
        wait_bytes(x_send.at[c, pl.ds(0, n_seq - 1)], xs_sem.at[c])
        if c > 0:
            wait_bytes(k_send.at[c], ks_sem.at[c])

        @pl.when(partner(c) != head)
        def _():
            wait_bytes(z_send.at[c], zs_sem.at[c])

    @pl.loop(0, jobs)
    def _(j):
        wait_bytes(b_send.at[j, pl.ds(0, n_seq - 1)], bs_sem.at[j])

        @pl.loop(1, n_head)
        def _(i):
            block = (head + i) % n_head
            wait_bytes(s_send.at[block, j], ss_sem.at[block, j])


def finish(mine, residual, gain, out_res, out_norm):
    f32, bf16 = jnp.float32, jnp.bfloat16
    stream = (residual[...].astype(f32) + mine[...].astype(f32)).astype(bf16)
    out_res[...] = stream
    wide = stream.astype(f32)
    scale = lax.rsqrt(jnp.mean(wide * wide, axis=-1, keepdims=True) + 1e-06)
    out_norm[...] = (wide * scale * gain[...]).astype(bf16)


def local(qkv, residual, dest_row, source_row, doc_start, out_weight, norm_gain):
    n_seq = lax.axis_size("seq")
    n_head = lax.axis_size("head")
    tok, _ = qkv.shape
    depth, model = out_weight.shape
    cap = -(-max(2, 3 * tok // (2 * n_seq)) // 8) * 8
    jobs = 4
    cols = model // jobs
    bf16 = jnp.bfloat16
    dma = pltpu.SemaphoreType.DMA
    vmem = pl.BlockSpec(memory_space=pltpu.VMEM)
    mine = pl.pallas_call(
        functools.partial(kernel, n_seq, n_head, cap, jobs),
        out_shape=jax.ShapeDtypeStruct(residual.shape, bf16),
        in_specs=[vmem, vmem, vmem, vmem, pl.BlockSpec(memory_space=pl.ANY)],
        out_specs=vmem,
        scratch_shapes=[
            pltpu.VMEM((depth, model), bf16),
            pltpu.VMEM((2, n_seq * 2 * cap, tok), bf16),
            pltpu.VMEM((2, tok, n_seq * 2 * cap), bf16),
            pltpu.VMEM((2, n_seq * 2 * cap, tok), bf16),
            pltpu.VMEM((2, tok, n_seq * 2 * cap), bf16),
            pltpu.VMEM((n_seq, 2 * cap, KVH * HD), bf16),
            pltpu.VMEM((n_seq, 2 * cap, KVH * HD), bf16),
            pltpu.VMEM((n_head, n_seq, 2 * cap, depth // 2), bf16),
            pltpu.VMEM((n_head, n_seq, 2 * cap, depth // 2), bf16),
            pltpu.VMEM((tok, 2 * KVH * HD), bf16),
            pltpu.VMEM((n_head, tok, 2 * HD), bf16),
            pltpu.VMEM((n_head, tok, 2 * HD), bf16),
            pltpu.VMEM((n_head, tok, depth), bf16),
            pltpu.VMEM((n_head, tok, depth), bf16),
            pltpu.VMEM((n_head, tok, depth), bf16),
            pltpu.VMEM((n_head, jobs, tok, cols), bf16),
            pltpu.VMEM((n_head + 1, jobs, tok, cols), bf16),
            pltpu.VMEM((tok, cols), jnp.float32),
            pltpu.VMEM((jobs, n_seq, 2 * cap, cols // 2), bf16),
            pltpu.VMEM((jobs, n_seq, 2 * cap, cols // 2), bf16),
            dma,
            dma,
            dma,
            dma((n_head,)),
            dma((n_head,)),
            dma((n_head,)),
            dma((n_head,)),
            dma((n_head,)),
            dma((n_head,)),
            dma((n_head, jobs)),
            dma((n_head + 1, jobs)),
            dma((jobs,)),
            dma((jobs,)),
        ],
        compiler_params=pltpu.CompilerParams(
            collective_id=0, has_side_effects=True, vmem_limit_bytes=56 * 1024 * 1024
        ),
        name="layer",
    )(
        qkv,
        dest_row.reshape(1, tok),
        source_row.reshape(1, tok),
        doc_start.reshape(1, tok * n_head),
        out_weight,
    )
    return pl.pallas_call(
        finish,
        out_shape=(jax.ShapeDtypeStruct(residual.shape, bf16), jax.ShapeDtypeStruct(residual.shape, bf16)),
        compiler_params=pltpu.CompilerParams(vmem_limit_bytes=16 * 1024 * 1024),
        name="finish",
    )(mine, residual, norm_gain.reshape(1, model))


def solution(mesh):
    return jax.shard_map(
        local,
        mesh=mesh,
        in_specs=(
            P(("seq", "head"), None),
            P(("seq", "head"), None),
            P(("seq", "head")),
            P(("seq", "head")),
            P("seq"),
            P("head", None),
            P(),
        ),
        out_specs=(P(("seq", "head"), None), P(("seq", "head"), None)),
        check_vma=False,
    )
```

time: 99.2 us -> 92.6 us (0.933)
  Pallas kernels: 93.6 us -> 89.8 us
  local copies, waits for them, and re-layouts: 3.76 us -> 1.04 us
    pallas_call x1, Pallas kernels: 93.6 us -> 88.7 us  [local(): pl.pallas_call(functools.partial(kernel, n_seq, n_head, cap, jobs), out_s...]
    unnamed x2 -> x6, local copies, waits for them, and re-layouts: 3.76 us -> 1.04 us
    pallas_call x0 -> x1, Pallas kernels: none -> 1.13 us  [local(): pl.pallas_call(finish, out_shape=(jax.ShapeDtypeStruct(residual.shape, bf...]
where the time goes in v2:
time: 92.6 us; the launch traced here: 91.5 us
  Pallas kernels  89.8 us (97%)
  local copies, waits for them, and re-layouts  1.04 us (1%)
    pallas_call x1, Pallas kernels, local(): pl.pallas_call(functools.partial(kernel, n_seq, n_head, cap, jobs), out_s...  88.7 us

profile of v2, /device:TPU:11, one launch (start us, length us, event | category | flops | bytes accessed | tf_op | source)
XLA Modules:
  0.0 91.5 jit_solution(9334544429340806447)
XLA Ops:
  0.6 0.0 copy-start.2
  0.6 0.0 copy-start.1
  0.7 88.7 %layer.1.mine = bf16[128,2048]{1,0:T(8,128)(2,1)} custom-call(bf16[128,4096]{1,0:T(8,128)(2,1)} %qkv.1, s32[1,128]{1,0:T(1,128)} %bitcast.6, s32[1,128]{1,0:T(1,128)} %bitcast.7, s32[1,512]{1,0:T(1,128)} %bitcast.5, bf16[768,2048]{1,0:T(8,128)(2,1)} %weight.1), custom_call_target="tpu_custom_call" | custom-call | tf_op jit(solution)/shard_map/layer/pallas_call | solution.py:307
  89.3 0.0 copy-done.2
  89.3 0.0 copy-done.1
  89.4 0.0 copy-start
  89.4 1.0 %copy-done = bf16[128,2048]{1,0:T(8,128)(2,1)S(1)} copy-done((bf16[128,2048]{1,0:T(8,128)(2,1)S(1)}, bf16[128,2048]{1,0:T(8,128)(2,1)}, u32[]{:S(2)}) %copy-start) | copy-done | bytes 524312
  90.4 1.1 %finish.1 = (bf16[128,2048]{1,0:T(8,128)(2,1)}, bf16[128,2048]{1,0:T(8,128)(2,1)}) custom-call(bf16[128,2048]{1,0:T(8,128)(2,1)S(1)} %copy-done, bf16[128,2048]{1,0:T(8,128)(2,1)S(1)} %copy-done.1, f32[1,2048]{1,0:T(1,128)S(1)} %bitcast.4), custom_call_target="tpu_custom_call" | custom-call | tf_op jit(solution)/shard_map/finish/pallas_call | solution.py:358
Async XLA Ops:
  0.6 88.7 %copy-start.2 = (f32[2048]{0:T(1024)S(1)}, f32[2048]{0:T(1024)}, u32[]{:S(2)}) copy-start(f32[2048]{0:T(1024)} %param.13) | copy-start | bytes 24580
  0.6 88.7 %copy-start.1 = (bf16[128,2048]{1,0:T(8,128)(2,1)S(1)}, bf16[128,2048]{1,0:T(8,128)(2,1)}, u32[]{:S(2)}) copy-start(bf16[128,2048]{1,0:T(8,128)(2,1)} %residual.1) | copy-start | bytes 1572868
  89.4 1.0 %copy-start = (bf16[128,2048]{1,0:T(8,128)(2,1)S(1)}, bf16[128,2048]{1,0:T(8,128)(2,1)}, u32[]{:S(2)}) copy-start(bf16[128,2048]{1,0:T(8,128)(2,1)} %layer.1.mine) | copy-start | bytes 1572868

commit v3 on v2

--- a/solution.py
+++ b/solution.py
@@ -106,10 +106,11 @@
     r_one[0], r_one[1] = rlow.astype(bf16), rhigh.astype(bf16)
     rt_one[0], rt_one[1] = rlow.T.astype(bf16), rhigh.T.astype(bf16)
 
-    for c in range(n_head):
+    def place_query(c):
         query = qkv[:, pl.ds(pl.multiple_of(partner(c) * depth, HD), depth)]
         place(query, x_send.at[c], x_recv.at[c], xs_sem.at[c], xr_sem.at[c])
 
+    place_query(0)
     kv_rows[...] = gather(kx_recv, kxr_sem)
 
     def kv_of(block):
@@ -129,6 +130,8 @@
         ).start()
 
     for c in range(n_head):
+        if c + 1 < n_head:
+            place_query(c + 1)
         rows = gather(x_recv.at[c], xr_sem.at[c])
         to = partner(c)
         z_send[c] = rows
@@ -193,11 +196,18 @@
 
     end = (head == 0) | (head == n_head - 1)
 
+    def chain(block):
+        @pl.loop(0, jobs)
+        def _(j):
+            step(block, j)
+
+    order = [0, n_head - 1] + list(range(1, n_head - 1))
+
     @pl.loop(0, n_head)
     def _(t):
-        block = partner(n_head - 1)
-        for c in range(n_head - 1):
-            block = jnp.where(t == c, partner(c), block)
+        block = partner(order[0])
+        for place_in, c in enumerate(order):
+            block = jnp.where(t == place_in, partner(c), block)
 
         @pl.when(block != head)
         def _():
@@ -208,25 +218,36 @@
 
         @pl.when((block != head) & end)
         def _():
-            @pl.loop(0, jobs)
-            def _(j):
-                step(block, j)
-
-    @pl.when(jnp.logical_not(end))
-    def _():
-        @pl.loop(0, n_head - 1)
-        def _(t):
-            above, below = n_head - 1 - t, t
-
-            @pl.loop(0, jobs)
-            def _(j):
-                @pl.when(above > head)
-                def _():
-                    step(above, j)
-
-                @pl.when(below < head)
-                def _():
-                    step(below, j)
+            chain(block)
+
+        if n_head == 4:
+
+            @pl.when(jnp.logical_not(end) & (t == 2))
+            def _():
+                chain(partner(1))
+                chain(partner(0))
+
+            @pl.when(jnp.logical_not(end) & (t == 3))
+            def _():
+                chain(partner(2))
+
+    if n_head != 4:
+
+        @pl.when(jnp.logical_not(end))
+        def _():
+            @pl.loop(0, n_head - 1)
+            def _(t):
+                above, below = n_head - 1 - t, t
+
+                @pl.loop(0, jobs)
+                def _(j):
+                    @pl.when(above > head)
+                    def _():
+                        step(above, j)
+
+                    @pl.when(below < head)
+                    def _():
+                        step(below, j)
 
     quarter = cols // 2
 

time: 92.6 us -> 80 us (0.86)
  the two profiles are of different devices: /device:TPU:11 before, /device:TPU:0 now
where the time goes in v3:
time: 80 us; the launch traced here: 79.8 us
  Pallas kernels  78.1 us (98%)
  local copies, waits for them, and re-layouts  1.04 us (1%)
    pallas_call x1, Pallas kernels, local(): pl.pallas_call(functools.partial(kernel, n_seq, n_head, cap, jobs), out_s...  77 us

profile of v3, /device:TPU:0, one launch (start us, length us, event | category | flops | bytes accessed | tf_op | source)
XLA Modules:
  0.0 79.8 jit_solution(14720915601344919436)
XLA Ops:
  0.6 0.0 copy-start.2
  0.6 0.0 copy-start.1
  0.7 77.0 %layer.1.mine = bf16[128,2048]{1,0:T(8,128)(2,1)} custom-call(bf16[128,4096]{1,0:T(8,128)(2,1)} %qkv.1, s32[1,128]{1,0:T(1,128)} %bitcast.6, s32[1,128]{1,0:T(1,128)} %bitcast.7, s32[1,512]{1,0:T(1,128)} %bitcast.5, bf16[768,2048]{1,0:T(8,128)(2,1)} %weight.1), custom_call_target="tpu_custom_call" | custom-call | tf_op jit(solution)/shard_map/layer/pallas_call | solution.py:328
  77.6 0.0 copy-done.2
  77.6 0.0 copy-done.1
  77.6 0.0 copy-start
  77.7 1.0 %copy-done = bf16[128,2048]{1,0:T(8,128)(2,1)S(1)} copy-done((bf16[128,2048]{1,0:T(8,128)(2,1)S(1)}, bf16[128,2048]{1,0:T(8,128)(2,1)}, u32[]{:S(2)}) %copy-start) | copy-done | bytes 524312
  78.7 1.1 %finish.1 = (bf16[128,2048]{1,0:T(8,128)(2,1)}, bf16[128,2048]{1,0:T(8,128)(2,1)}) custom-call(bf16[128,2048]{1,0:T(8,128)(2,1)S(1)} %copy-done, bf16[128,2048]{1,0:T(8,128)(2,1)S(1)} %copy-done.1, f32[1,2048]{1,0:T(1,128)S(1)} %bitcast.4), custom_call_target="tpu_custom_call" | custom-call | tf_op jit(solution)/shard_map/finish/pallas_call | solution.py:379
Async XLA Ops:
  0.6 77.0 %copy-start.2 = (f32[2048]{0:T(1024)S(1)}, f32[2048]{0:T(1024)}, u32[]{:S(2)}) copy-start(f32[2048]{0:T(1024)} %param.13) | copy-start | bytes 24580
  0.6 77.0 %copy-start.1 = (bf16[128,2048]{1,0:T(8,128)(2,1)S(1)}, bf16[128,2048]{1,0:T(8,128)(2,1)}, u32[]{:S(2)}) copy-start(bf16[128,2048]{1,0:T(8,128)(2,1)} %residual.1) | copy-start | bytes 1572868
  77.6 1.0 %copy-start = (bf16[128,2048]{1,0:T(8,128)(2,1)S(1)}, bf16[128,2048]{1,0:T(8,128)(2,1)}, u32[]{:S(2)}) copy-start(bf16[128,2048]{1,0:T(8,128)(2,1)} %layer.1.mine) | copy-start | bytes 1572868

commit v4 on v3

--- a/solution.py
+++ b/solution.py
@@ -25,11 +25,11 @@
 
 def kernel(
     n_seq, n_head, cap, jobs,
-    qkv, dest, source, starts, weight,
+    qkv_hbm, dest, source, starts, weight,
     out,
-    w_vmem, p_one, pt_one, r_one, rt_one, kx_send, kx_recv, x_send, x_recv, kv_rows, k_send, kv_recv,
+    qkv, w_vmem, p_one, pt_one, r_one, rt_one, kx_send, kx_recv, x_send, x_recv, kv_rows, k_send, kv_recv,
     z_send, q_recv, attn, s_send, s_recv, acc, b_send, b_recv,
-    w_sem, kxs_sem, kxr_sem, xs_sem, xr_sem, ks_sem, kr_sem, zs_sem, zr_sem, ss_sem, sr_sem, bs_sem, br_sem,
+    in_sem, w_sem, kxs_sem, kxr_sem, xs_sem, xr_sem, ks_sem, kr_sem, zs_sem, zr_sem, ss_sem, sr_sem, bs_sem, br_sem,
 ):
     f32, bf16 = jnp.float32, jnp.bfloat16
     seq, head = lax.axis_index("seq"), lax.axis_index("head")
@@ -46,8 +46,13 @@
     def wait_bytes(ref, sem):
         pltpu.make_async_copy(ref, ref, sem).wait()
 
+    loads = [
+        pltpu.make_async_copy(qkv_hbm.at[:, part], qkv.at[:, part], in_sem.at[at])
+        for at, part in enumerate((slice(QH * HD, None), slice(0, QH * HD)))
+    ]
+    for load in loads:
+        load.start()
     load_w = pltpu.make_async_copy(weight, w_vmem, w_sem)
-    load_w.start()
 
     barrier = pltpu.get_barrier_semaphore()
 
@@ -96,6 +101,7 @@
 
     shifts = [(n_head - 1 + c) % n_head for c in range(n_head)]
     depth = heads_here * HD
+    loads[0].wait()
     place(qkv[:, QH * HD :], kx_send, kx_recv, kxs_sem, kxr_sem)
 
     low_t, high_t = low.T, high.T
@@ -110,6 +116,8 @@
         query = qkv[:, pl.ds(pl.multiple_of(partner(c) * depth, HD), depth)]
         place(query, x_send.at[c], x_recv.at[c], xs_sem.at[c], xr_sem.at[c])
 
+    loads[1].wait()
+    load_w.start()
     place_query(0)
     kv_rows[...] = gather(kx_recv, kxr_sem)
 
@@ -201,58 +209,9 @@
         def _(j):
             step(block, j)
 
-    order = [0, n_head - 1] + list(range(1, n_head - 1))
-
-    @pl.loop(0, n_head)
-    def _(t):
-        block = partner(order[0])
-        for place_in, c in enumerate(order):
-            block = jnp.where(t == place_in, partner(c), block)
-
-        @pl.when(block != head)
-        def _():
-            wait_bytes(q_recv.at[block], zr_sem.at[block])
-
-        for i in range(n_head):
-            pl.when(block == i)(functools.partial(attend, i))
-
-        @pl.when((block != head) & end)
-        def _():
-            chain(block)
-
-        if n_head == 4:
-
-            @pl.when(jnp.logical_not(end) & (t == 2))
-            def _():
-                chain(partner(1))
-                chain(partner(0))
-
-            @pl.when(jnp.logical_not(end) & (t == 3))
-            def _():
-                chain(partner(2))
-
-    if n_head != 4:
-
-        @pl.when(jnp.logical_not(end))
-        def _():
-            @pl.loop(0, n_head - 1)
-            def _(t):
-                above, below = n_head - 1 - t, t
-
-                @pl.loop(0, jobs)
-                def _(j):
-                    @pl.when(above > head)
-                    def _():
-                        step(above, j)
-
-                    @pl.when(below < head)
-                    def _():
-                        step(below, j)
-
     quarter = cols // 2
 
-    @pl.loop(0, jobs)
-    def _(j):
+    def own(j):
         acc[...] = partial(head, j)
 
         @pl.when(head > 0)
@@ -279,6 +238,100 @@
                 device_id=(peer, head), device_id_type=MESH,
             ).start()
 
+    def paced(c, j):
+        older = partner(c) if c == 0 else jnp.where(j >= 2, partner(c), partner(c - 1))
+        at = (j + jobs - 2) % jobs
+        wait_bytes(s_send.at[older, at], ss_sem.at[older, at])
+        step(partner(c), j)
+
+    order = [0, n_head - 1] + list(range(1, n_head - 1))
+
+    @pl.loop(0, n_head)
+    def _(t):
+        block = partner(order[0])
+        for place_in, c in enumerate(order):
+            block = jnp.where(t == place_in, partner(c), block)
+
+        @pl.when(block != head)
+        def _():
+            wait_bytes(q_recv.at[block], zr_sem.at[block])
+
+        for i in range(n_head):
+            pl.when(block == i)(functools.partial(attend, i))
+
+        if n_head != 4:
+
+            @pl.when((block != head) & end)
+            def _():
+                chain(block)
+        else:
+
+            @pl.when(end & (t == 0))
+            def _():
+                @pl.loop(0, 2)
+                def _(j):
+                    step(partner(0), j)
+
+            @pl.when(end & (t == 1))
+            def _():
+                @pl.loop(2, jobs)
+                def _(j):
+                    paced(0, j)
+
+            @pl.when(end & (t == 2))
+            def _():
+                @pl.loop(0, 2)
+                def _(j):
+                    paced(1, j)
+
+    if n_head == 4:
+
+        @pl.when(end)
+        def _():
+            @pl.loop(2, jobs)
+            def _(j):
+                paced(1, j)
+
+            @pl.loop(0, jobs)
+            def _(j):
+                paced(2, j)
+                own(j)
+
+        @pl.when(jnp.logical_not(end))
+        def _():
+            @pl.loop(0, jobs)
+            def _(j):
+                step(partner(1), j)
+                step(partner(2), j)
+
+            chain(partner(0))
+
+            @pl.loop(0, jobs)
+            def _(j):
+                own(j)
+
+    else:
+
+        @pl.when(jnp.logical_not(end))
+        def _():
+            @pl.loop(0, n_head - 1)
+            def _(t):
+                above, below = n_head - 1 - t, t
+
+                @pl.loop(0, jobs)
+                def _(j):
+                    @pl.when(above > head)
+                    def _():
+                        step(above, j)
+
+                    @pl.when(below < head)
+                    def _():
+                        step(below, j)
+
+        @pl.loop(0, jobs)
+        def _(j):
+            own(j)
+
     for j in range(jobs):
         wait_bytes(b_recv.at[j, pl.ds(0, n_seq - 1)], br_sem.at[j])
         arrived = b_recv[j].reshape(slots, quarter)
@@ -302,7 +355,11 @@
         @pl.loop(1, n_head)
         def _(i):
             block = (head + i) % n_head
-            wait_bytes(s_send.at[block, j], ss_sem.at[block, j])
+            left = (block == partner(n_head - 2)) & (j >= jobs - 2) if n_head == 4 else block != head
+
+            @pl.when(jnp.logical_not(end) | left)
+            def _():
+                wait_bytes(s_send.at[block, j], ss_sem.at[block, j])
 
 
 def finish(mine, residual, gain, out_res, out_norm):
@@ -325,46 +382,50 @@
     bf16 = jnp.bfloat16
     dma = pltpu.SemaphoreType.DMA
     vmem = pl.BlockSpec(memory_space=pltpu.VMEM)
+    hbm = pl.BlockSpec(memory_space=pltpu.HBM)
+    scratch = [
+        pltpu.VMEM(qkv.shape, bf16),
+        pltpu.VMEM((depth, model), bf16),
+        pltpu.VMEM((2, n_seq * 2 * cap, tok), bf16),
+        pltpu.VMEM((2, tok, n_seq * 2 * cap), bf16),
+        pltpu.VMEM((2, n_seq * 2 * cap, tok), bf16),
+        pltpu.VMEM((2, tok, n_seq * 2 * cap), bf16),
+        pltpu.VMEM((n_seq, 2 * cap, KVH * HD), bf16),
+        pltpu.VMEM((n_seq, 2 * cap, KVH * HD), bf16),
+        pltpu.VMEM((n_head, n_seq, 2 * cap, depth // 2), bf16),
+        pltpu.VMEM((n_head, n_seq, 2 * cap, depth // 2), bf16),
+        pltpu.VMEM((tok, 2 * KVH * HD), bf16),
+        pltpu.VMEM((n_head, tok, 2 * HD), bf16),
+        pltpu.VMEM((n_head, tok, 2 * HD), bf16),
+        pltpu.VMEM((n_head, tok, depth), bf16),
+        pltpu.VMEM((n_head, tok, depth), bf16),
+        pltpu.VMEM((n_head, tok, depth), bf16),
+        pltpu.VMEM((n_head, jobs, tok, cols), bf16),
+        pltpu.VMEM((n_head + 1, jobs, tok, cols), bf16),
+        pltpu.VMEM((tok, cols), jnp.float32),
+        pltpu.VMEM((jobs, n_seq, 2 * cap, cols // 2), bf16),
+        pltpu.VMEM((jobs, n_seq, 2 * cap, cols // 2), bf16),
+        dma((2,)),
+        dma,
+        dma,
+        dma,
+        dma((n_head,)),
+        dma((n_head,)),
+        dma((n_head,)),
+        dma((n_head,)),
+        dma((n_head,)),
+        dma((n_head,)),
+        dma((n_head, jobs)),
+        dma((n_head + 1, jobs)),
+        dma((jobs,)),
+        dma((jobs,)),
+    ]
     mine = pl.pallas_call(
         functools.partial(kernel, n_seq, n_head, cap, jobs),
         out_shape=jax.ShapeDtypeStruct(residual.shape, bf16),
-        in_specs=[vmem, vmem, vmem, vmem, pl.BlockSpec(memory_space=pl.ANY)],
+        in_specs=[hbm, vmem, vmem, vmem, hbm],
         out_specs=vmem,
-        scratch_shapes=[
-            pltpu.VMEM((depth, model), bf16),
-            pltpu.VMEM((2, n_seq * 2 * cap, tok), bf16),
-            pltpu.VMEM((2, tok, n_seq * 2 * cap), bf16),
-            pltpu.VMEM((2, n_seq * 2 * cap, tok), bf16),
-            pltpu.VMEM((2, tok, n_seq * 2 * cap), bf16),
-            pltpu.VMEM((n_seq, 2 * cap, KVH * HD), bf16),
-            pltpu.VMEM((n_seq, 2 * cap, KVH * HD), bf16),
-            pltpu.VMEM((n_head, n_seq, 2 * cap, depth // 2), bf16),
-            pltpu.VMEM((n_head, n_seq, 2 * cap, depth // 2), bf16),
-            pltpu.VMEM((tok, 2 * KVH * HD), bf16),
-            pltpu.VMEM((n_head, tok, 2 * HD), bf16),
-            pltpu.VMEM((n_head, tok, 2 * HD), bf16),
-            pltpu.VMEM((n_head, tok, depth), bf16),
-            pltpu.VMEM((n_head, tok, depth), bf16),
-            pltpu.VMEM((n_head, tok, depth), bf16),
-            pltpu.VMEM((n_head, jobs, tok, cols), bf16),
-            pltpu.VMEM((n_head + 1, jobs, tok, cols), bf16),
-            pltpu.VMEM((tok, cols), jnp.float32),
-            pltpu.VMEM((jobs, n_seq, 2 * cap, cols // 2), bf16),
-            pltpu.VMEM((jobs, n_seq, 2 * cap, cols // 2), bf16),
-            dma,
-            dma,
-            dma,
-            dma((n_head,)),
-            dma((n_head,)),
-            dma((n_head,)),
-            dma((n_head,)),
-            dma((n_head,)),
-            dma((n_head,)),
-            dma((n_head, jobs)),
-            dma((n_head + 1, jobs)),
-            dma((jobs,)),
-            dma((jobs,)),
-        ],
+        scratch_shapes=scratch,
         compiler_params=pltpu.CompilerParams(
             collective_id=0, has_side_effects=True, vmem_limit_bytes=56 * 1024 * 1024
         ),

time: 80 us -> 78.1 us (0.976)
  the two profiles are of different devices: /device:TPU:0 before, /device:TPU:11 now
where the time goes in v4:
time: 78.1 us; the launch traced here: 77.9 us
  Pallas kernels  76.2 us (98%)
  local copies, waits for them, and re-layouts  1.04 us (1%)
    pallas_call x1, Pallas kernels, local(): pl.pallas_call(functools.partial(kernel, n_seq, n_head, cap, jobs), out_s...  75.1 us

profile of v4, /device:TPU:11, one launch (start us, length us, event | category | flops | bytes accessed | tf_op | source)
XLA Modules:
  0.0 77.9 jit_solution(4232894341301784606)
XLA Ops:
  0.6 0.0 copy-start.2
  0.6 0.0 copy-start.1
  0.7 75.1 %layer.1.mine = bf16[128,2048]{1,0:T(8,128)(2,1)} custom-call(bf16[128,4096]{1,0:T(8,128)(2,1)} %qkv_hbm.1, s32[1,128]{1,0:T(1,128)} %bitcast.6, s32[1,128]{1,0:T(1,128)} %bitcast.7, s32[1,512]{1,0:T(1,128)} %bitcast.5, bf16[768,2048]{1,0:T(8,128)(2,1)} %weight.1), custom_call_target="tpu_custom_call" | custom-call | tf_op jit(solution)/shard_map/layer/pallas_call | solution.py:423
  75.7 0.0 copy-done.2
  75.7 0.0 copy-done.1
  75.7 0.0 copy-start
  75.8 1.0 %copy-done = bf16[128,2048]{1,0:T(8,128)(2,1)S(1)} copy-done((bf16[128,2048]{1,0:T(8,128)(2,1)S(1)}, bf16[128,2048]{1,0:T(8,128)(2,1)}, u32[]{:S(2)}) %copy-start) | copy-done | bytes 524312
  76.8 1.1 %finish.1 = (bf16[128,2048]{1,0:T(8,128)(2,1)}, bf16[128,2048]{1,0:T(8,128)(2,1)}) custom-call(bf16[128,2048]{1,0:T(8,128)(2,1)S(1)} %copy-done, bf16[128,2048]{1,0:T(8,128)(2,1)S(1)} %copy-done.1, f32[1,2048]{1,0:T(1,128)S(1)} %bitcast.4), custom_call_target="tpu_custom_call" | custom-call | tf_op jit(solution)/shard_map/finish/pallas_call | solution.py:440
Async XLA Ops:
  0.6 75.1 %copy-start.2 = (f32[2048]{0:T(1024)S(1)}, f32[2048]{0:T(1024)}, u32[]{:S(2)}) copy-start(f32[2048]{0:T(1024)} %param.13) | copy-start | bytes 24580
  0.6 75.1 %copy-start.1 = (bf16[128,2048]{1,0:T(8,128)(2,1)S(1)}, bf16[128,2048]{1,0:T(8,128)(2,1)}, u32[]{:S(2)}) copy-start(bf16[128,2048]{1,0:T(8,128)(2,1)} %residual.1) | copy-start | bytes 1572868
  75.7 1.0 %copy-start = (bf16[128,2048]{1,0:T(8,128)(2,1)S(1)}, bf16[128,2048]{1,0:T(8,128)(2,1)}, u32[]{:S(2)}) copy-start(bf16[128,2048]{1,0:T(8,128)(2,1)} %layer.1.mine) | copy-start | bytes 1572868

commit v5 on v4

--- a/solution.py
+++ b/solution.py
@@ -76,7 +76,7 @@
     def partner(c):
         if n_head == 4:
             mirror = n_head - 1 - head
-            return [mirror, (head + 2) % n_head, (mirror + 2) % n_head, head][c]
+            return [(mirror + 2) % n_head, mirror, (head + 2) % n_head, head][c]
         return (shifts[c] - head + n_head) % n_head
 
     def place(x, send, recv, s_sem, r_sem):
@@ -104,21 +104,19 @@
     loads[0].wait()
     place(qkv[:, QH * HD :], kx_send, kx_recv, kxs_sem, kxr_sem)
 
-    low_t, high_t = low.T, high.T
-    pt_one[0], pt_one[1] = low_t.astype(bf16), high_t.astype(bf16)
+    def place_query(c):
+        query = qkv[:, pl.ds(pl.multiple_of(partner(c) * depth, HD), depth)]
+        place(query, x_send.at[c], x_recv.at[c], xs_sem.at[c], xr_sem.at[c])
+
+    loads[1].wait()
+    load_w.start()
+    place_query(0)
+
     across = jnp.broadcast_to(source[...].astype(f32), (tok, tok))
     before = (across.T < across).astype(f32).astype(bf16)
     rlow, rhigh = one_hot_slots(comes, dot(comes.astype(f32).astype(bf16), before), n_seq, cap)
     r_one[0], r_one[1] = rlow.astype(bf16), rhigh.astype(bf16)
     rt_one[0], rt_one[1] = rlow.T.astype(bf16), rhigh.T.astype(bf16)
-
-    def place_query(c):
-        query = qkv[:, pl.ds(pl.multiple_of(partner(c) * depth, HD), depth)]
-        place(query, x_send.at[c], x_recv.at[c], xs_sem.at[c], xr_sem.at[c])
-
-    loads[1].wait()
-    load_w.start()
-    place_query(0)
     kv_rows[...] = gather(kx_recv, kxr_sem)
 
     def kv_of(block):
@@ -140,6 +138,8 @@
     for c in range(n_head):
         if c + 1 < n_head:
             place_query(c + 1)
+        if c == n_head - 1 and n_head == 4:
+            continue
         rows = gather(x_recv.at[c], xr_sem.at[c])
         to = partner(c)
         z_send[c] = rows
@@ -252,6 +252,13 @@
         for place_in, c in enumerate(order):
             block = jnp.where(t == place_in, partner(c), block)
 
+        @pl.when(t == 1)
+        def _():
+            for side in range(2):
+                pt_one[side] = p_one[side].astype(f32).T.astype(bf16)
+            if n_head == 4:
+                q_recv[pl.ds(head, 1)] = gather(x_recv.at[n_head - 1], xr_sem.at[n_head - 1])[None]
+
         @pl.when(block != head)
         def _():
             wait_bytes(q_recv.at[block], zr_sem.at[block])
@@ -301,10 +308,10 @@
         def _():
             @pl.loop(0, jobs)
             def _(j):
-                step(partner(1), j)
                 step(partner(2), j)
-
-            chain(partner(0))
+                step(partner(0), j)
+
+            chain(partner(1))
 
             @pl.loop(0, jobs)
             def _(j):
@@ -427,7 +434,7 @@
         out_specs=vmem,
         scratch_shapes=scratch,
         compiler_params=pltpu.CompilerParams(
-            collective_id=0, has_side_effects=True, vmem_limit_bytes=56 * 1024 * 1024
+            collective_id=0, has_side_effects=True, vmem_limit_bytes=54 * 1024 * 1024
         ),
         name="layer",
     )(

time: 78.1 us -> 85.2 us (1.091)
  Pallas kernels: 76.2 us -> 83.3 us
    pallas_call x1, Pallas kernels: 75.1 us -> 82.1 us  [local(): pl.pallas_call(functools.partial(kernel, n_seq, n_head, cap, jobs), out_s...]
where the time goes in v5:
time: 85.2 us; the launch traced here: 85 us
  Pallas kernels  83.3 us (98%)
  local copies, waits for them, and re-layouts  1.04 us (1%)
    pallas_call x1, Pallas kernels, local(): pl.pallas_call(functools.partial(kernel, n_seq, n_head, cap, jobs), out_s...  82.1 us

profile of v5, /device:TPU:11, one launch (start us, length us, event | category | flops | bytes accessed | tf_op | source)
XLA Modules:
  0.0 85.0 jit_solution(10172410812801668047)
XLA Ops:
  0.6 0.0 copy-start.2
  0.6 0.0 copy-start.1
  0.7 82.1 %layer.1.mine = bf16[128,2048]{1,0:T(8,128)(2,1)} custom-call(bf16[128,4096]{1,0:T(8,128)(2,1)} %qkv_hbm.1, s32[1,128]{1,0:T(1,128)} %bitcast.6, s32[1,128]{1,0:T(1,128)} %bitcast.7, s32[1,512]{1,0:T(1,128)} %bitcast.5, bf16[768,2048]{1,0:T(8,128)(2,1)} %weight.1), custom_call_target="tpu_custom_call" | custom-call | tf_op jit(solution)/shard_map/layer/pallas_call | solution.py:430
  82.8 0.0 copy-done.2
  82.8 0.0 copy-done.1
  82.8 0.0 copy-start
  82.8 1.0 %copy-done = bf16[128,2048]{1,0:T(8,128)(2,1)S(1)} copy-done((bf16[128,2048]{1,0:T(8,128)(2,1)S(1)}, bf16[128,2048]{1,0:T(8,128)(2,1)}, u32[]{:S(2)}) %copy-start) | copy-done | bytes 524312
  83.9 1.1 %finish.1 = (bf16[128,2048]{1,0:T(8,128)(2,1)}, bf16[128,2048]{1,0:T(8,128)(2,1)}) custom-call(bf16[128,2048]{1,0:T(8,128)(2,1)S(1)} %copy-done, bf16[128,2048]{1,0:T(8,128)(2,1)S(1)} %copy-done.1, f32[1,2048]{1,0:T(1,128)S(1)} %bitcast.4), custom_call_target="tpu_custom_call" | custom-call | tf_op jit(solution)/shard_map/finish/pallas_call | solution.py:447
Async XLA Ops:
  0.6 82.2 %copy-start.2 = (f32[2048]{0:T(1024)S(1)}, f32[2048]{0:T(1024)}, u32[]{:S(2)}) copy-start(f32[2048]{0:T(1024)} %param.13) | copy-start | bytes 24580
  0.6 82.2 %copy-start.1 = (bf16[128,2048]{1,0:T(8,128)(2,1)S(1)}, bf16[128,2048]{1,0:T(8,128)(2,1)}, u32[]{:S(2)}) copy-start(bf16[128,2048]{1,0:T(8,128)(2,1)} %residual.1) | copy-start | bytes 1572868
  82.8 1.0 %copy-start = (bf16[128,2048]{1,0:T(8,128)(2,1)S(1)}, bf16[128,2048]{1,0:T(8,128)(2,1)}, u32[]{:S(2)}) copy-start(bf16[128,2048]{1,0:T(8,128)(2,1)} %layer.1.mine) | copy-start | bytes 1572868

commit v6 on v5

--- a/solution.py
+++ b/solution.py
@@ -76,7 +76,7 @@
     def partner(c):
         if n_head == 4:
             mirror = n_head - 1 - head
-            return [(mirror + 2) % n_head, mirror, (head + 2) % n_head, head][c]
+            return [mirror, (head + 2) % n_head, (mirror + 2) % n_head, head][c]
         return (shifts[c] - head + n_head) % n_head
 
     def place(x, send, recv, s_sem, r_sem):
@@ -308,10 +308,10 @@
         def _():
             @pl.loop(0, jobs)
             def _(j):
+                step(partner(1), j)
                 step(partner(2), j)
-                step(partner(0), j)
-
-            chain(partner(1))
+
+            chain(partner(0))
 
             @pl.loop(0, jobs)
             def _(j):
@@ -434,7 +434,7 @@
         out_specs=vmem,
         scratch_shapes=scratch,
         compiler_params=pltpu.CompilerParams(
-            collective_id=0, has_side_effects=True, vmem_limit_bytes=54 * 1024 * 1024
+            collective_id=0, has_side_effects=True, vmem_limit_bytes=56 * 1024 * 1024
         ),
         name="layer",
     )(

time: 85.2 us -> 78.4 us (0.920)
  Pallas kernels: 83.3 us -> 76.5 us
    pallas_call x1, Pallas kernels: 82.1 us -> 75.4 us  [local(): pl.pallas_call(functools.partial(kernel, n_seq, n_head, cap, jobs), out_s...]
where the time goes in v6:
time: 78.4 us; the launch traced here: 78.3 us
  Pallas kernels  76.5 us (98%)
  local copies, waits for them, and re-layouts  1.04 us (1%)
    pallas_call x1, Pallas kernels, local(): pl.pallas_call(functools.partial(kernel, n_seq, n_head, cap, jobs), out_s...  75.4 us

profile of v6, /device:TPU:11, one launch (start us, length us, event | category | flops | bytes accessed | tf_op | source)
XLA Modules:
  0.0 78.3 jit_solution(9067207915696371318)
XLA Ops:
  0.6 0.0 copy-start.2
  0.6 0.0 copy-start.1
  0.7 75.4 %layer.1.mine = bf16[128,2048]{1,0:T(8,128)(2,1)} custom-call(bf16[128,4096]{1,0:T(8,128)(2,1)} %qkv_hbm.1, s32[1,128]{1,0:T(1,128)} %bitcast.6, s32[1,128]{1,0:T(1,128)} %bitcast.7, s32[1,512]{1,0:T(1,128)} %bitcast.5, bf16[768,2048]{1,0:T(8,128)(2,1)} %weight.1), custom_call_target="tpu_custom_call" | custom-call | tf_op jit(solution)/shard_map/layer/pallas_call | solution.py:430
  76.1 0.0 copy-done.2
  76.1 0.0 copy-done.1
  76.1 0.0 copy-start
  76.1 1.0 %copy-done = bf16[128,2048]{1,0:T(8,128)(2,1)S(1)} copy-done((bf16[128,2048]{1,0:T(8,128)(2,1)S(1)}, bf16[128,2048]{1,0:T(8,128)(2,1)}, u32[]{:S(2)}) %copy-start) | copy-done | bytes 524312
  77.1 1.1 %finish.1 = (bf16[128,2048]{1,0:T(8,128)(2,1)}, bf16[128,2048]{1,0:T(8,128)(2,1)}) custom-call(bf16[128,2048]{1,0:T(8,128)(2,1)S(1)} %copy-done, bf16[128,2048]{1,0:T(8,128)(2,1)S(1)} %copy-done.1, f32[1,2048]{1,0:T(1,128)S(1)} %bitcast.4), custom_call_target="tpu_custom_call" | custom-call | tf_op jit(solution)/shard_map/finish/pallas_call | solution.py:447
Async XLA Ops:
  0.6 75.4 %copy-start.2 = (f32[2048]{0:T(1024)S(1)}, f32[2048]{0:T(1024)}, u32[]{:S(2)}) copy-start(f32[2048]{0:T(1024)} %param.13) | copy-start | bytes 24580
  0.6 75.4 %copy-start.1 = (bf16[128,2048]{1,0:T(8,128)(2,1)S(1)}, bf16[128,2048]{1,0:T(8,128)(2,1)}, u32[]{:S(2)}) copy-start(bf16[128,2048]{1,0:T(8,128)(2,1)} %residual.1) | copy-start | bytes 1572868
  76.1 1.0 %copy-start = (bf16[128,2048]{1,0:T(8,128)(2,1)S(1)}, bf16[128,2048]{1,0:T(8,128)(2,1)}, u32[]{:S(2)}) copy-start(bf16[128,2048]{1,0:T(8,128)(2,1)} %layer.1.mine) | copy-start | bytes 1572868

commit v7 on v4

--- a/solution.py
+++ b/solution.py
@@ -377,7 +377,7 @@
     tok, _ = qkv.shape
     depth, model = out_weight.shape
     cap = -(-max(2, 3 * tok // (2 * n_seq)) // 8) * 8
-    jobs = 4
+    jobs = 8
     cols = model // jobs
     bf16 = jnp.bfloat16
     dma = pltpu.SemaphoreType.DMA

time: 78.1 us -> 85.9 us (1.100)
  Pallas kernels: 76.2 us -> 84 us
    pallas_call x1, Pallas kernels: 75.1 us -> 82.8 us  [local(): pl.pallas_call(functools.partial(kernel, n_seq, n_head, cap, jobs), out_s...]
where the time goes in v7:
time: 85.9 us; the launch traced here: 85.7 us
  Pallas kernels  84 us (98%)
  local copies, waits for them, and re-layouts  1.04 us (1%)
    pallas_call x1, Pallas kernels, local(): pl.pallas_call(functools.partial(kernel, n_seq, n_head, cap, jobs), out_s...  82.8 us

profile of v7, /device:TPU:11, one launch (start us, length us, event | category | flops | bytes accessed | tf_op | source)
XLA Modules:
  0.0 85.7 jit_solution(8879035538445340091)
XLA Ops:
  0.6 0.0 copy-start.2
  0.6 0.0 copy-start.1
  0.7 82.8 %layer.1.mine = bf16[128,2048]{1,0:T(8,128)(2,1)} custom-call(bf16[128,4096]{1,0:T(8,128)(2,1)} %qkv_hbm.1, s32[1,128]{1,0:T(1,128)} %bitcast.6, s32[1,128]{1,0:T(1,128)} %bitcast.7, s32[1,512]{1,0:T(1,128)} %bitcast.5, bf16[768,2048]{1,0:T(8,128)(2,1)} %weight.1), custom_call_target="tpu_custom_call" | custom-call | tf_op jit(solution)/shard_map/layer/pallas_call | solution.py:423
  83.5 0.0 copy-done.2
  83.5 0.0 copy-done.1
  83.5 0.0 copy-start
  83.5 1.0 %copy-done = bf16[128,2048]{1,0:T(8,128)(2,1)S(1)} copy-done((bf16[128,2048]{1,0:T(8,128)(2,1)S(1)}, bf16[128,2048]{1,0:T(8,128)(2,1)}, u32[]{:S(2)}) %copy-start) | copy-done | bytes 524312
  84.6 1.1 %finish.1 = (bf16[128,2048]{1,0:T(8,128)(2,1)}, bf16[128,2048]{1,0:T(8,128)(2,1)}) custom-call(bf16[128,2048]{1,0:T(8,128)(2,1)S(1)} %copy-done, bf16[128,2048]{1,0:T(8,128)(2,1)S(1)} %copy-done.1, f32[1,2048]{1,0:T(1,128)S(1)} %bitcast.4), custom_call_target="tpu_custom_call" | custom-call | tf_op jit(solution)/shard_map/finish/pallas_call | solution.py:440
Async XLA Ops:
  0.6 82.9 %copy-start.2 = (f32[2048]{0:T(1024)S(1)}, f32[2048]{0:T(1024)}, u32[]{:S(2)}) copy-start(f32[2048]{0:T(1024)} %param.13) | copy-start | bytes 24580
  0.6 82.9 %copy-start.1 = (bf16[128,2048]{1,0:T(8,128)(2,1)S(1)}, bf16[128,2048]{1,0:T(8,128)(2,1)}, u32[]{:S(2)}) copy-start(bf16[128,2048]{1,0:T(8,128)(2,1)} %residual.1) | copy-start | bytes 1572868
  83.5 1.0 %copy-start = (bf16[128,2048]{1,0:T(8,128)(2,1)S(1)}, bf16[128,2048]{1,0:T(8,128)(2,1)}, u32[]{:S(2)}) copy-start(bf16[128,2048]{1,0:T(8,128)(2,1)} %layer.1.mine) | copy-start | bytes 1572868
